TPU v7x, 256 devices: a whole 4x4x8 slice. The times are simulated.
256 devices in a mesh: mem: 16 (over y, x), lat: 16 (over z, core).
Axes of the slice: x: 4, y: 4, z: 8, core: 2. Of those that a mesh axis runs over, the one named last changes fastest.
Arguments:
- prior_sample: bfloat16 [64, 83, 131072], P('mem', None, 'lat'), may hold values from -6 to 6
- measured_values: bfloat16 [65536], P('lat'), may hold values from -8 to 8
- measured_quantity: int32 [65536], P('lat'), may hold values from 0 to 82
- measured_vertical: int32 [65536], P('lat'), may hold values from 0 to 8191
- measure_position_matrix: int32 [512, 8192], P('mem', 'lat'), may hold values from 0 to 6143, as said below
- alive_slot_number: int32 [512, 16], P('mem', 'lat'), may hold values from 1 to 512, as said below
- tapered_precision_factor: float32 [512, 8192], P('mem', 'lat'), may hold values from 0.02 to 0.5
Outputs:
- analysis: bfloat16 [64, 83, 131072], P('mem', None, 'lat')
Inputs may be any that keep to these rules, and one draw needn't show every extreme that they name: `measure_position_matrix`: within a patch the indices are distinct and lie within 1024 consecutive window entries; patches of the first band never index below 1024, patches of the last band never index 5120 or above. `alive_slot_number`: every device holds a patch with exactly 512 live slots.
All inputs are finite; a program needn't handle non-finite values.
Results may differ from a plain program's by a relative error of at most 0.0046.
Values may be sent and summed in bfloat16 or wider, within the bound.
A program may use at most 128 MiB of HBM per device.

v0:
```python
import math

import jax
import jax.numpy as jnp
from jax import lax
from jax.sharding import PartitionSpec as P

NS_STEPS = 8
HALO = 1024


def extended(value, sides, width):
    for axis, dim in sides:
        size, length = (lax.axis_size(axis), value.shape[dim])
        up = [(i, (i + 1) % size) for i in range(size - 1)]
        down = [(j, i) for i, j in up]
        last = lax.slice_in_dim(value, length - width, length, axis=dim)
        first = lax.slice_in_dim(value, 0, width, axis=dim)
        before = lax.ppermute(last, axis, up)
        after = lax.ppermute(first, axis, down)
        value = jnp.concatenate([before, value, after], axis=dim)
    return value


def patch_weights(pert, depart, weight, counts):
    sample_fields = pert.shape[0]
    slots = pert.shape[2]
    live = jnp.arange(slots, dtype=jnp.int32)[None, :] < counts[:, None]
    rweight = jnp.where(live, weight, jnp.zeros_like(weight))
    scaled = pert * rweight[None, :, :]
    identity = jnp.eye(sample_fields, dtype=pert.dtype)
    gram = (
        jnp.einsum("jpl,kpl->pjk", pert, scaled, precision=lax.Precision.HIGHEST)
        + (sample_fields - 1.0) * identity
    )
    trace_sum = jnp.trace(gram, axis1=1, axis2=2)
    root = gram / trace_sum[:, None, None]
    inverse = jnp.broadcast_to(identity, root.shape)
    for sweep in range(NS_STEPS):
        middle = 0.5 * (3.0 * identity - jnp.matmul(inverse, root, precision=lax.Precision.HIGHEST))
        root = jnp.matmul(root, middle, precision=lax.Precision.HIGHEST)
        inverse = jnp.matmul(middle, inverse, precision=lax.Precision.HIGHEST)
    spread = inverse * (jnp.sqrt(sample_fields - 1.0) / jnp.sqrt(trace_sum))[:, None, None]
    covar = jnp.matmul(inverse, inverse, precision=lax.Precision.HIGHEST) / trace_sum[:, None, None]
    project = jnp.einsum("jpl,pl->pj", scaled, depart, precision=lax.Precision.HIGHEST)
    shift = jnp.einsum("pjk,pk->pj", covar, project, precision=lax.Precision.HIGHEST)
    full = spread + shift[:, :, None]
    return (full + (1.0 - jnp.sum(full, axis=1, keepdims=True)) / sample_fields).astype(
        jnp.bfloat16
    )


def pick_slots(rows_bf, mean, lists):
    window = rows_bf.shape[1]
    slots = lists.shape[1]
    reach_cols = min(2 * slots, window)
    offsets = jnp.arange(reach_cols, dtype=jnp.int32)

    def one_patch(slot_index):
        first_col = jnp.minimum(jnp.min(slot_index), window - reach_cols)
        window_part = lax.dynamic_slice_in_dim(rows_bf, first_col, reach_cols, 1)
        mean_part = lax.dynamic_slice_in_dim(mean, first_col, reach_cols, 0)
        selector = (first_col + offsets)[:, None] == slot_index[None, :]
        picked = jnp.dot(
            window_part, selector.astype(jnp.bfloat16), preferred_element_type=jnp.float32
        )
        picked_mean = jnp.dot(
            mean_part[None, :], selector.astype(jnp.float32), precision=lax.Precision.HIGHEST
        )[0]
        return (picked, picked_mean)

    patches = lists.shape[0]
    block_size = math.gcd(patches, 8)
    grouped = lists.reshape(patches // block_size, block_size, slots)
    picked, picked_mean = lax.map(jax.vmap(one_patch), grouped)
    picked = picked.reshape(patches, rows_bf.shape[0], slots)
    picked_mean = picked_mean.reshape(patches, slots)
    return (picked, picked_mean)


def on_device(
    prior_sample,
    measured_values,
    measured_quantity,
    measured_vertical,
    measure_position_matrix,
    alive_slot_number,
    tapered_precision_factor,
):
    tile_samples, quantity_number, verticals_in_strip = prior_sample.shape
    band_groups = lax.axis_size("mem")
    sample_fields = tile_samples * band_groups
    linear_field_vector = prior_sample.reshape(tile_samples, quantity_number * verticals_in_strip)
    equiv = jnp.take(
        linear_field_vector, measured_quantity * verticals_in_strip + measured_vertical, axis=1
    )
    every_own = lax.all_gather(equiv, "mem", axis=0, tiled=True)
    stacked = jnp.concatenate([every_own, measured_values[None, :]], axis=0)
    widened = extended(stacked, (("lat", 1),), HALO)
    every = widened[:sample_fields]
    observed = widened[sample_fields]
    mean = jnp.sum(every.astype(jnp.float32), axis=0) / sample_fields
    all_rows = jnp.concatenate([every, observed[None, :]], axis=0)
    picked, picked_mean = pick_slots(all_rows, mean, measure_position_matrix)
    ylocal = jnp.transpose(picked[:, :sample_fields, :] - picked_mean[:, None, :], (1, 0, 2))
    dlocal = picked[:, sample_fields, :] - picked_mean
    weights = patch_weights(ylocal, dlocal, tapered_precision_factor, alive_slot_number[:, 0])
    patches = measure_position_matrix.shape[0]
    width = verticals_in_strip // (patches * band_groups)
    tile_pieces = prior_sample.reshape(
        tile_samples, quantity_number, band_groups, verticals_in_strip // band_groups
    )
    mine = lax.all_to_all(tile_pieces, "mem", split_axis=2, concat_axis=0, tiled=True)
    columns = mine.reshape(sample_fields, quantity_number, patches, width)
    result = jnp.einsum("jvpc,pjk->kvpc", columns, weights, preferred_element_type=jnp.float32)
    result = result.astype(jnp.bfloat16).reshape(sample_fields, quantity_number, 1, patches * width)
    back = lax.all_to_all(result, "mem", split_axis=0, concat_axis=2, tiled=True)
    return back.reshape(tile_samples, quantity_number, verticals_in_strip)


def solution(mesh):
    placed = (
        P("mem", None, "lat"),
        P("lat"),
        P("lat"),
        P("lat"),
        P("mem", "lat"),
        P("mem", "lat"),
        P("mem", "lat"),
    )
    return jax.shard_map(
        on_device, mesh=mesh, in_specs=placed, out_specs=P("mem", None, "lat"), check_vma=False
    )
```

profile of v0, /device:TPU:96, one launch (start us, length us, event | category | flops | bytes accessed | tf_op | source)
XLA Modules:
  0.0 409.7 jit_solution(7565916927658990750)
XLA Ops:
  1.5 49.6 %gather_fusion = bf16[4096,4]{0,1:T(4,128)(2,1)S(1)} fusion(bf16[4,679936]{1,0:T(4,128)(2,1)} %bitcast.159, s32[4096]{0:T(1024)S(1)} %broadcast_clamp_fusion), kind=kCustom, calls=%fused_computation | custom fusion | bytes 81920 | tf_op jit(solution)/shard_map/jit(_take)/gather | solution.py:94
  51.2 24.3 %all-gather = bf16[16,4,4096]{2,1,0:T(4,128)(2,1)S(1)} all-gather(bf16[1,4,4096]{2,1,0:T(4,128)(2,1)S(1)} %select_bitcast_fusion), channel_id=1, replica_groups=mesh['mem'=16,'lat'=16] {'mem'}, dimensions={0}, use_global_device_ids=true | all-gather | bytes 557056 | tf_op jit(solution)/shard_map/all_gather | solution.py:97
  75.7 1.9 collective-permute-start
  77.6 3.6 collective-permute-start.1
  81.2 6.8 %copy.45 = bf16[83,1,16,4,512]{4,3,1,0,2:T(4,128)(2,1)} copy(bf16[83,1,16,4,512]{4,3,2,1,0:T(4,128)(2,1)} %bitcast.160) | data formatting | bytes 10878976 | tf_op jit(solution)/shard_map/reshape | solution.py:110
  88.1 5.1 %all-to-all-start = ((bf16[4,83,16,512]{3,0,1,2:T(4,128)(2,1)}), bf16[4,83,16,512]{3,0,1,2:T(4,128)(2,1)}, u32[]{:S(2)}, u32[]{:S(2)}) async-start(bf16[4,83,16,512]{3,0,1,2:T(4,128)(2,1)} %bitcast.158), calls=%async_computation | async-start | bytes 10878976 | tf_op jit(solution)/shard_map/all_to_all | solution.py:113
  93.6 136.4 %while.21 = (s32[]{:T(128)}, f32[4,8,65,512]{3,2,1,0:T(8,128)}, f32[4,8,512]{2,1,0:T(8,128)S(1)}, s32[4,8,512]{2,1,0:T(8,128)}, bf16[65,6144]{1,0:T(8,128)(2,1)S...) while((s32[]{:T(128)}, f32[4,8,65,512]{3,2,1,0:T(8,128)}, ...), condition=%wide.region_3.4_spmd.clone, body=%wide.region_1.3_spmd.clone.sunk | while | flops 603992128 | bytes 2802391 | solution.py:75
  94.6 12.1 %while.23 = (s32[]{:T(128)}, f32[6144]{0:T(1024)S(1)}, s32[8,1]{0,1:T(1,128)S(1)}, f32[8,1024]{1,0:T(8,128)S(1)}, s32[]{:T(128)}, /*index=5*/s32[]{:T(128)}) while((s32[]{:T(128)}, f32[6144]{0:T(1024)S(1)}, s32[8,1]{0,1:T(1,128)S(1)}, f32[8,1024]{1,0:T(8,128)S(1)}, s32[]{:T(128)}, /*index=5*/s32[]{:T(128)}) %tuple.61), condition=%wide.while_cond.1, body=%wide.while_body.1.sunk | while | flops 2 | bytes 16481 | solution.py:62
  106.7 5.4 %fusion.134 = f32[8,1,512]{2,1,0:T(1,128)S(1)} fusion(s32[8,512]{1,0:T(8,128)S(1)} %get-tuple-element.212, s32[8,1024]{1,0:T(8,128)S(1)} %iota_add_fusion.2, f32[8,1024,1]{1,0,2:T(8,128)S(1)} %bitcast.168), kind=kOutput, calls=%fused_computation.5.clone.1 | convolution fusion | flops 54525952 | bytes 98304 | tf_op jit(solution)/shard_map/while/body/eval_jaxpr/vmap()/dot_general | solution.py:67
  112.1 11.3 %while.22 = (s32[]{:T(128)}, bf16[65,6144]{1,0:T(8,128)(2,1)S(1)}, s32[8,2]{0,1:T(2,128)S(1)}, bf16[8,65,1024]{2,1,0:T(8,128)(2,1)S(1)}, s32[]{:T(128)}) while((s32[]{:T(128)}, bf16[65,6144]{1,0:T(8,128)(2,1)S(1)}, s32[8,2]{0,1:T(2,128)S(1)}, bf16[8,65,1024]{2,1,0:T(8,128)(2,1)S(1)}, s32[]{:T(128)}) %tuple.58), condition=%wide.while_cond, body=%wide.while_body.sunk | while | flops 2 | bytes 295017 | solution.py:61
  123.5 4.2 %fusion.133 = f32[4,8,65,512]{3,2,1,0:T(8,128)} fusion(f32[4,8,65,512]{3,2,1,0:T(8,128)} %get-tuple-element.268, s32[]{:T(128)S(6)} %copy.70, bf16[8,65,1024]{2,1,0:T(8,128)(2,1)S(1)} %get-tuple-element.211, s32[8,512]{1,0:T(8,128)S(1)} %get-tuple-element.212, s32[8,1024]{1,0:T(8,128)S(1)} %iota_add_fusion.2), kind=kOutput, calls=%fused_computation.14.clone.1 | convolution fusion | flops 549453824 | bytes 2293764 | tf_op jit(solution)/shard_map/while/body/eval_jaxpr/vmap()/dot_general | solution.py:64
  128.6 12.1 %while.23 = (s32[]{:T(128)}, f32[6144]{0:T(1024)S(1)}, s32[8,1]{0,1:T(1,128)S(1)}, f32[8,1024]{1,0:T(8,128)S(1)}, s32[]{:T(128)}, /*index=5*/s32[]{:T(128)}) while((s32[]{:T(128)}, f32[6144]{0:T(1024)S(1)}, s32[8,1]{0,1:T(1,128)S(1)}, f32[8,1024]{1,0:T(8,128)S(1)}, s32[]{:T(128)}, /*index=5*/s32[]{:T(128)}) %tuple.61), condition=%wide.while_cond.1, body=%wide.while_body.1.sunk | while | flops 2 | bytes 16481 | solution.py:62
  140.8 5.4 %fusion.134 = f32[8,1,512]{2,1,0:T(1,128)S(1)} fusion(s32[8,512]{1,0:T(8,128)S(1)} %get-tuple-element.212, s32[8,1024]{1,0:T(8,128)S(1)} %iota_add_fusion.2, f32[8,1024,1]{1,0,2:T(8,128)S(1)} %bitcast.168), kind=kOutput, calls=%fused_computation.5.clone.1 | convolution fusion | flops 54525952 | bytes 98304 | tf_op jit(solution)/shard_map/while/body/eval_jaxpr/vmap()/dot_general | solution.py:67
  146.2 11.3 %while.22 = (s32[]{:T(128)}, bf16[65,6144]{1,0:T(8,128)(2,1)S(1)}, s32[8,2]{0,1:T(2,128)S(1)}, bf16[8,65,1024]{2,1,0:T(8,128)(2,1)S(1)}, s32[]{:T(128)}) while((s32[]{:T(128)}, bf16[65,6144]{1,0:T(8,128)(2,1)S(1)}, s32[8,2]{0,1:T(2,128)S(1)}, bf16[8,65,1024]{2,1,0:T(8,128)(2,1)S(1)}, s32[]{:T(128)}) %tuple.58), condition=%wide.while_cond, body=%wide.while_body.sunk | while | flops 2 | bytes 295017 | solution.py:61
  157.5 4.2 %fusion.133 = f32[4,8,65,512]{3,2,1,0:T(8,128)} fusion(f32[4,8,65,512]{3,2,1,0:T(8,128)} %get-tuple-element.268, s32[]{:T(128)S(6)} %copy.70, bf16[8,65,1024]{2,1,0:T(8,128)(2,1)S(1)} %get-tuple-element.211, s32[8,512]{1,0:T(8,128)S(1)} %get-tuple-element.212, s32[8,1024]{1,0:T(8,128)S(1)} %iota_add_fusion.2), kind=kOutput, calls=%fused_computation.14.clone.1 | convolution fusion | flops 549453824 | bytes 2293764 | tf_op jit(solution)/shard_map/while/body/eval_jaxpr/vmap()/dot_general | solution.py:64
  162.7 12.1 %while.23 = (s32[]{:T(128)}, f32[6144]{0:T(1024)S(1)}, s32[8,1]{0,1:T(1,128)S(1)}, f32[8,1024]{1,0:T(8,128)S(1)}, s32[]{:T(128)}, /*index=5*/s32[]{:T(128)}) while((s32[]{:T(128)}, f32[6144]{0:T(1024)S(1)}, s32[8,1]{0,1:T(1,128)S(1)}, f32[8,1024]{1,0:T(8,128)S(1)}, s32[]{:T(128)}, /*index=5*/s32[]{:T(128)}) %tuple.61), condition=%wide.while_cond.1, body=%wide.while_body.1.sunk | while | flops 2 | bytes 16481 | solution.py:62
  174.8 5.4 %fusion.134 = f32[8,1,512]{2,1,0:T(1,128)S(1)} fusion(s32[8,512]{1,0:T(8,128)S(1)} %get-tuple-element.212, s32[8,1024]{1,0:T(8,128)S(1)} %iota_add_fusion.2, f32[8,1024,1]{1,0,2:T(8,128)S(1)} %bitcast.168), kind=kOutput, calls=%fused_computation.5.clone.1 | convolution fusion | flops 54525952 | bytes 98304 | tf_op jit(solution)/shard_map/while/body/eval_jaxpr/vmap()/dot_general | solution.py:67
  180.2 11.3 %while.22 = (s32[]{:T(128)}, bf16[65,6144]{1,0:T(8,128)(2,1)S(1)}, s32[8,2]{0,1:T(2,128)S(1)}, bf16[8,65,1024]{2,1,0:T(8,128)(2,1)S(1)}, s32[]{:T(128)}) while((s32[]{:T(128)}, bf16[65,6144]{1,0:T(8,128)(2,1)S(1)}, s32[8,2]{0,1:T(2,128)S(1)}, bf16[8,65,1024]{2,1,0:T(8,128)(2,1)S(1)}, s32[]{:T(128)}) %tuple.58), condition=%wide.while_cond, body=%wide.while_body.sunk | while | flops 2 | bytes 295017 | solution.py:61
  191.6 4.2 %fusion.133 = f32[4,8,65,512]{3,2,1,0:T(8,128)} fusion(f32[4,8,65,512]{3,2,1,0:T(8,128)} %get-tuple-element.268, s32[]{:T(128)S(6)} %copy.70, bf16[8,65,1024]{2,1,0:T(8,128)(2,1)S(1)} %get-tuple-element.211, s32[8,512]{1,0:T(8,128)S(1)} %get-tuple-element.212, s32[8,1024]{1,0:T(8,128)S(1)} %iota_add_fusion.2), kind=kOutput, calls=%fused_computation.14.clone.1 | convolution fusion | flops 549453824 | bytes 2293764 | tf_op jit(solution)/shard_map/while/body/eval_jaxpr/vmap()/dot_general | solution.py:64
  196.7 12.1 %while.23 = (s32[]{:T(128)}, f32[6144]{0:T(1024)S(1)}, s32[8,1]{0,1:T(1,128)S(1)}, f32[8,1024]{1,0:T(8,128)S(1)}, s32[]{:T(128)}, /*index=5*/s32[]{:T(128)}) while((s32[]{:T(128)}, f32[6144]{0:T(1024)S(1)}, s32[8,1]{0,1:T(1,128)S(1)}, f32[8,1024]{1,0:T(8,128)S(1)}, s32[]{:T(128)}, /*index=5*/s32[]{:T(128)}) %tuple.61), condition=%wide.while_cond.1, body=%wide.while_body.1.sunk | while | flops 2 | bytes 16481 | solution.py:62
  208.9 5.4 %fusion.134 = f32[8,1,512]{2,1,0:T(1,128)S(1)} fusion(s32[8,512]{1,0:T(8,128)S(1)} %get-tuple-element.212, s32[8,1024]{1,0:T(8,128)S(1)} %iota_add_fusion.2, f32[8,1024,1]{1,0,2:T(8,128)S(1)} %bitcast.168), kind=kOutput, calls=%fused_computation.5.clone.1 | convolution fusion | flops 54525952 | bytes 98304 | tf_op jit(solution)/shard_map/while/body/eval_jaxpr/vmap()/dot_general | solution.py:67
  214.3 11.3 %while.22 = (s32[]{:T(128)}, bf16[65,6144]{1,0:T(8,128)(2,1)S(1)}, s32[8,2]{0,1:T(2,128)S(1)}, bf16[8,65,1024]{2,1,0:T(8,128)(2,1)S(1)}, s32[]{:T(128)}) while((s32[]{:T(128)}, bf16[65,6144]{1,0:T(8,128)(2,1)S(1)}, s32[8,2]{0,1:T(2,128)S(1)}, bf16[8,65,1024]{2,1,0:T(8,128)(2,1)S(1)}, s32[]{:T(128)}) %tuple.58), condition=%wide.while_cond, body=%wide.while_body.sunk | while | flops 2 | bytes 295017 | solution.py:61
  225.6 4.2 %fusion.133 = f32[4,8,65,512]{3,2,1,0:T(8,128)} fusion(f32[4,8,65,512]{3,2,1,0:T(8,128)} %get-tuple-element.268, s32[]{:T(128)S(6)} %copy.70, bf16[8,65,1024]{2,1,0:T(8,128)(2,1)S(1)} %get-tuple-element.211, s32[8,512]{1,0:T(8,128)S(1)} %get-tuple-element.212, s32[8,1024]{1,0:T(8,128)S(1)} %iota_add_fusion.2), kind=kOutput, calls=%fused_computation.14.clone.1 | convolution fusion | flops 549453824 | bytes 2293764 | tf_op jit(solution)/shard_map/while/body/eval_jaxpr/vmap()/dot_general | solution.py:64
  231.1 7.9 %select_reduce_fusion = (f32[32]{0:T(128)S(1)}, f32[32,64,64]{2,1,0:T(8,128)S(1)}) fusion(pred[64,64]{1,0:T(8,128)(4,1)S(1)} %iota_compare_fusion.1, f32[64,64]{1,0:T(8,128)S(1)} %fusion.57, f32[32,65,512]{2,1,0:T(8,128)} %bitcast.151, f32[32,512]{1,0:T(8,128)S(1)} %fusion.56, f32[32,512]{1,0:T(8,128)S(1)} %bitcast.162), kind=kOutput, calls=%fused_computation.56 | convolution fusion | flops 808845312 | bytes 9150592 | tf_op jit(solution)/shard_map/jpl,kpl->pjk/dot_general | solution.py:33
  268.8 4.1 fusion.41
  272.8 1.7 fusion.74
  275.0 17.4 %copy.23 = bf16[16,4,83,1,512]{2,1,0,4,3:T(4,128)(2,1)} copy(bf16[16,4,83,1,512]{4,1,2,0,3:T(4,128)(2,1)} %bitcast.17) | data formatting | bytes 10878976 | tf_op jit(solution)/shard_map/all_to_all | solution.py:113
  292.5 9.7 %convolution_convert_fusion = bf16[32,64,83,16]{2,1,3,0:T(8,128)(2,1)} fusion(bf16[64,83,32,16]{1,0,3,2:T(8,128)(2,1)} %bitcast.156, f32[32,64,64]{2,1,0:T(8,128)S(1)} %fusion.73, f32[32,64]{1,0:T(8,128)S(1)} %subtract_multiply_fusion, f32[32,64]{1,0:T(8,128)S(1)} %bitcast.165, f32[32]{0:T(128)S(1)} %rsqrt_multiply_fusion), kind=kOutput, calls=%fused_computation.22 | convolution fusion | flops 351371264 | bytes 11419776 | tf_op jit(solution)/shard_map/jvpc,pjk->kvpc/dot_general | solution.py:115
  302.2 12.7 %copy.25 = bf16[64,83,1,512]{3,1,2,0:T(8,128)(2,1)} copy(bf16[64,83,1,512]{1,0,3,2:T(8,128)(2,1)} %bitcast.155) | data formatting | bytes 10878976 | tf_op jit(solution)/shard_map/reshape | solution.py:116
  314.9 76.9 %all_to_all.30 = bf16[64,83,1,512]{3,1,2,0:T(8,128)(2,1)S(1)} all-to-all(bf16[64,83,1,512]{3,1,2,0:T(8,128)(2,1)} %copy.25), channel_id=1, replica_groups=mesh['mem'=16,'lat'=16] {'mem'}, dimensions={0} | all-to-all | bytes 10878976 | tf_op jit(solution)/shard_map/all_to_all | solution.py:117
  391.8 5.5 %copy.26 = bf16[4,83,16,1,512]{4,2,0,1,3:T(8,128)(2,1)} copy(bf16[4,83,16,1,512]{4,1,0,2,3:T(8,128)(2,1)S(1)} %bitcast.157) | data formatting | bytes 10878976 | tf_op jit(solution)/shard_map/all_to_all | solution.py:117
  397.3 12.2 %reshape.115 = bf16[4,83,8192]{2,0,1:T(4,128)(2,1)} reshape(bf16[4,83,16,1,512]{4,2,0,1,3:T(8,128)(2,1)} %copy.26) | data formatting | bytes 10878976 | tf_op jit(solution)/shard_map/reshape | solution.py:118
  (284 shorter events, 129.3 us)
Async XLA Ops:
  0.0 75.6 %copy-start.1 = (bf16[4096]{0:T(1024)(128)(2,1)S(1)}, bf16[4096]{0:T(1024)(128)(2,1)}, u32[]{:S(2)}) copy-start(bf16[4096]{0:T(1024)(128)(2,1)} %param.10) | copy-start | bytes 24580
  75.7 17.7 %collective-permute-start = (bf16[65,1024]{1,0:T(8,128)(2,1)S(1)}, bf16[65,1024]{1,0:T(8,128)(2,1)S(1)}, u32[]{:S(2)}, u32[]{:S(2)}) collective-permute-start(bf16[65,1024]{1,0:T(8,128)(2,1)S(1)} %get-tuple-element.107), channel_id=1, source_target_pairs={{0,1},{1,2},{2,3},{3,4},{4,5},{5,6},{6,7},{7,8},{8,9},{9,10},{10,1... | collective-permute-start | bytes 399368 | tf_op jit(solution)/shard_map/ppermute | solution.py:19
  77.6 15.8 %collective-permute-start.1 = (bf16[65,1024]{1,0:T(8,128)(2,1)S(1)}, bf16[65,1024]{1,0:T(8,128)(2,1)S(1)}, u32[]{:S(2)}, u32[]{:S(2)}) collective-permute-start(bf16[65,1024]{1,0:T(8,128)(2,1)S(1)} %get-tuple-element.108), channel_id=1, source_target_pairs={{1,0},{2,1},{3,2},{4,3},{5,4},{6,5},{7,6},{8,7},{9,8},{10,9},{11,1... | collective-permute-start | bytes 399368 | tf_op jit(solution)/shard_map/ppermute | solution.py:20
  88.1 5.2 %copy-start = (f32[32,512]{1,0:T(8,128)S(1)}, f32[32,512]{1,0:T(8,128)}, u32[]{:S(2)}) copy-start(f32[32,512]{1,0:T(8,128)} %param.15) | copy-start | bytes 196612
  88.1 5.2 %copy-start.2 = (s32[32,1]{0,1:T(1,128)S(1)}, s32[32,1]{0,1:T(1,128)}, u32[]{:S(2)}) copy-start(s32[32,1]{0,1:T(1,128)} %param.14) | copy-start | bytes 388
  88.1 187.0 %all-to-all-start = ((bf16[4,83,16,512]{3,0,1,2:T(4,128)(2,1)}), bf16[4,83,16,512]{3,0,1,2:T(4,128)(2,1)}, u32[]{:S(2)}, u32[]{:S(2)}) async-start(bf16[4,83,16,512]{3,0,1,2:T(4,128)(2,1)} %bitcast.158), calls=%async_computation | async-start | bytes 10878976 | tf_op jit(solution)/shard_map/all_to_all | solution.py:113
  262.7 6.1 %slice-start = ((s8[4718592]{0:T(1024)(128)(4,1)}), s8[4194304]{0:T(1024)(128)(4,1)S(1)}, s32[]{:S(2)}) async-start(s8[4718592]{0:T(1024)(128)(4,1)} %bitcast.152), calls=%async_computation.2 | async-start | bytes 8388608
  265.1 3.7 slice-start.1
where the time goes:
time: 418 us; the launch traced here: 410 us
  local copies, waits for them, and re-layouts  198 us (47%)
  blocking collectives  101 us (24%)
  matrix products  91.4 us (22%)
  starting transfers between devices  10.7 us (3%)
  other arithmetic  6 us (1%)
    gather x192, local copies, waits for them, and re-layouts  92.5 us
    all_to_all x1, blocking collectives, on_device(): lax.all_to_all(result, 'mem', split_axis=0, concat_axis=2, tiled=True)  76.9 us
    gather x1, local copies, waits for them, and re-layouts, on_device(): jnp.take(linear_field_vector, measured_quantity * verticals_in_strip + me...  49.6 us
    all_gather x1, blocking collectives, on_device(): every_own = lax.all_gather(equiv, 'mem', axis=0, tiled=True)  24.3 us
    dot_general x4, matrix products, one_patch(): jnp.dot(mean_part[None, :], selector.astype(jnp.float32), precision=lax.P...  21.6 us
    all_to_all x1, local copies, waits for them, and re-layouts, on_device(): lax.all_to_all(tile_pieces, 'mem', split_axis=2, concat_axis=0, tiled=True)  17.4 us
    dot_general x4, matrix products, one_patch(): jnp.dot(window_part, selector.astype(jnp.bfloat16), preferred_element_typ...  16.9 us
    reshape x1, local copies, waits for them, and re-layouts, on_device(): result.astype(jnp.bfloat16)  12.7 us
  transfers between devices with their start and end apart: 3, of which 0 were waited for; matrix products, arithmetic and copies ran while one was open for 46% of the time, Pallas kernels for 0%

commit v1 on v0

v1 whole, which is shorter than its diff:
```python
import functools
import math

import jax
import jax.numpy as jnp
from jax import lax
from jax.experimental import pallas as pl
from jax.experimental.pallas import tpu as pltpu
from jax.sharding import PartitionSpec as P

MESH = pl.DeviceIdType.MESH
F32, BF16 = jnp.float32, jnp.bfloat16

MEMBERS = 64
MINE = 4
NV = 83
NVP = 88
BAND = 8192
OWN = 512
NG = 4
PATCHES = 32
SLOTS = 512
SPAN = 9
NWT = 48
NOT = 32
NS_STEPS = 8
PAIRS = PATCHES // 2
BATCH = 8
ROWS = (NVP // 8) * (BAND // 128) * 8

ORDER = (
    (1, 0), (0, 2), (3, 0), (2, 1), (0, 1), (2, 3), (0, 3), (1, 2),
    (2, 0), (3, 2), (1, 1), (3, 3), (2, 2), (1, 3), (3, 1),
)


def dot(a, b):
    return jnp.dot(a, b, preferred_element_type=F32)


def dot_t(a, b):
    return lax.dot_general(a, b, (((1,), (1,)), ((), ())), preferred_element_type=F32)


def halves(value):
    high = value.astype(BF16)
    return high, (value - high.astype(F32)).astype(BF16)


def left(value):
    rows = jnp.concatenate(halves(value), axis=0)
    return jnp.concatenate([rows, rows], axis=1)


def right(value, block_mask):
    high, low = halves(value)
    return jnp.concatenate(
        [
            jnp.concatenate([high, high], axis=0) * block_mask,
            jnp.concatenate([low, low], axis=0) * block_mask,
        ],
        axis=0,
    )


def folded(product):
    half = product.shape[0] // 2
    return product[:half] + product[half:]


def kernel(
    prior, spots, columns, tiles, alive, values, lists, taper,
    out,
    mine, table, alone, got, made, equiv32, equiv, every, window, perts, value_win, parts, depart,
    gram, proj, weights, wide, wide_out,
    own_sem, in_send, in_recv, in_own, gather_send, gather_recv, gather_own,
    halo_send, halo_recv, value_send, value_recv, value_own, out_send, out_recv, out_own,
):
    me, lat = lax.axis_index("mem"), lax.axis_index("lat")
    bands = lax.axis_size("lat")
    my_y, my_x = me // 4, me % 4
    partners = [((my_y + dy) % 4) * 4 + (my_x + dx) % 4 for dx, dy in ORDER]
    north, south = (lat + 1) % bands, (lat + bands - 1) % bands

    load = [
        pltpu.make_async_copy(prior.at[j], mine.at[j], own_sem.at[j]) for j in range(MINE)
    ]
    for copy in load:
        copy.start()

    barrier = pltpu.get_barrier_semaphore()
    for partner in partners:
        pl.semaphore_signal(barrier, inc=1, device_id=(partner, lat), device_id_type=MESH)
    for band in (north, south):
        pl.semaphore_signal(barrier, inc=1, device_id=(me, band), device_id_type=MESH)
    pl.semaphore_wait(barrier, len(ORDER) + 2)

    def piece(owner, group):
        return pl.ds(pl.multiple_of(owner * OWN + group * 128, 128), 128)

    my_rows = pl.ds(me * MINE, MINE)

    def copies_in(group):
        sends = [
            pltpu.make_async_remote_copy(
                src_ref=prior.at[:, :, piece(partner, group)],
                dst_ref=got.at[group, my_rows],
                send_sem=in_send.at[group, s],
                recv_sem=in_recv.at[group, s],
                device_id=(partner, lat),
                device_id_type=MESH,
            )
            for s, partner in enumerate(partners)
        ]
        own = pltpu.make_async_copy(
            prior.at[:, :, piece(me, group)], got.at[group, my_rows], in_own.at[group]
        )
        return sends + [own]

    def copies_out(group):
        sends = [
            pltpu.make_async_remote_copy(
                src_ref=made.at[group, pl.ds(partner * MINE, MINE)],
                dst_ref=out.at[:, :, piece(me, group)],
                send_sem=out_send.at[group, s],
                recv_sem=out_recv.at[group, s],
                device_id=(partner, lat),
                device_id_type=MESH,
            )
            for s, partner in enumerate(partners)
        ]
        own = pltpu.make_async_copy(
            made.at[group, my_rows], out.at[:, :, piece(me, group)], out_own.at[group]
        )
        return sends + [own]

    ins = [copies_in(group) for group in range(NG)]
    outs = [copies_out(group) for group in range(NG)]
    for copy in ins[0]:
        copy.start()

    value_copies = [
        pltpu.make_async_remote_copy(
            src_ref=values.at[source],
            dst_ref=value_win.at[target],
            send_sem=value_send.at[k],
            recv_sem=value_recv.at[k],
            device_id=(me, band),
            device_id_type=MESH,
        )
        for k, (source, target, band) in enumerate(((3, 0, north), (0, 5, south)))
    ]
    value_copies.append(pltpu.make_async_copy(values, value_win.at[pl.ds(1, 4)], value_own))
    for copy in value_copies:
        copy.start()

    for copy in load:
        copy.wait()

    def spread_rows(ct, carry):
        lanes = pl.ds(pl.multiple_of(ct * 128, 128), 128)
        for j in range(MINE):
            for v in range(0, NV, 16):
                count = min(16, NV - v)
                block = mine[j, v : v + count, lanes].astype(F32)
                for t in range(0, count, 8):
                    n = min(8, count - t)
                    start = (((v + t) // 8) * (BAND // 128) + ct) * 8 * MINE + j
                    table[pl.ds(start, n, stride=MINE), :] = block[t : t + n]
        return carry

    lax.fori_loop(0, BAND // 128, spread_rows, 0)

    lane4 = lax.broadcasted_iota(jnp.int32, (MINE, 128), 1)
    ones = jnp.ones((8, 128), BF16)

    def pick(ot, carry):
        for i in range(128):
            found = table[pl.ds(spots[ot * 128 + i], MINE), :]
            alone[pl.ds(i, MINE, stride=128), :] = jnp.where(
                lane4 == columns[ot * 128 + i], found, 0.0
            )
        row = dot_t(ones, alone[...].astype(BF16))
        start = (ot // 8) * 8 * MINE + ot % 8
        for j in range(MINE):
            equiv32[pl.ds(start + j * 8, 1), :] = row[0:1, j * 128 : j * 128 + 128]
        return carry

    lax.fori_loop(0, NOT, pick, 0)
    for quarter in range(4):
        equiv[quarter] = equiv32[quarter * 32 : quarter * 32 + 32].astype(BF16)

    gathers = [
        pltpu.make_async_remote_copy(
            src_ref=equiv,
            dst_ref=every.at[pl.ds(1, 4), me],
            send_sem=gather_send.at[s],
            recv_sem=gather_recv.at[s],
            device_id=(partner, lat),
            device_id_type=MESH,
        )
        for s, partner in enumerate(partners)
    ]
    gathers.append(pltpu.make_async_copy(equiv, every.at[pl.ds(1, 4), me], gather_own))
    for copy in gathers:
        copy.start()
    for group in range(1, NG):
        for copy in ins[group]:
            copy.start()
    for copy in gathers:
        copy.wait()
    halos = [
        pltpu.make_async_remote_copy(
            src_ref=every.at[source],
            dst_ref=every.at[target],
            send_sem=halo_send.at[k],
            recv_sem=halo_recv.at[k],
            device_id=(me, band),
            device_id_type=MESH,
        )
        for k, (source, target, band) in enumerate(((4, 0, north), (1, 5, south)))
    ]
    for copy in halos:
        copy.start()

    def spread_members(q, carry):
        for m in range(MEMBERS // MINE):
            block = every[q, m].astype(F32)
            for j in range(MINE):
                start = q * 8 * MEMBERS + m * MINE + j
                window[pl.ds(start, 8, stride=MEMBERS), :] = block[j * 8 : j * 8 + 8]
        return carry

    def center(tile, carry):
        rows = pl.ds(pl.multiple_of(tile * MEMBERS, MEMBERS), MEMBERS)
        field = window[rows, :]
        mean = jnp.sum(field, axis=0, keepdims=True) * (1.0 / MEMBERS)
        pert = field - mean
        perts[tile] = pert
        parts[tile] = jnp.concatenate(halves(pert), axis=0)
        depart[pl.ds(tile, 1), :] = value_win[tile // 8, pl.ds(tile % 8, 1), :] - mean
        return carry

    for copy in value_copies:
        copy.wait()
    lax.fori_loop(1, 5, spread_members, 0)
    lax.fori_loop(8, 40, center, 0)
    for copy in halos:
        copy.wait()
    for quarter in (0, 5):
        spread_members(quarter, 0)
        lax.fori_loop(quarter * 8, quarter * 8 + 8, center, 0)

    slot = lax.broadcasted_iota(jnp.int32, (1, SLOTS), 1)
    high_row = lax.broadcasted_iota(jnp.int32, (16, SLOTS), 0)
    low_row = lax.broadcasted_iota(jnp.int32, (128, SLOTS), 0)
    lane64 = lax.broadcasted_iota(jnp.int32, (MEMBERS, 128), 1)
    row64 = lax.broadcasted_iota(jnp.int32, (MEMBERS, 128), 0)
    first_half = lane64 < MEMBERS
    diagonal = (lane64 % MEMBERS) == row64
    unit = diagonal.astype(F32)
    first_lane = lax.broadcasted_iota(jnp.int32, (1, 128), 1) < MEMBERS

    def one_patch(p):
        base = tiles[p]
        place = lists[pl.ds(p, 1), :] - base * 128
        weight = jnp.where(slot < alive[p], taper[pl.ds(p, 1), :], 0.0)
        hit = high_row == lax.shift_right_arithmetic(place, 7)
        laid = []
        rest = weight
        for _ in range(3):
            part = rest.astype(BF16).astype(F32)
            laid.append(jnp.where(hit, part, 0.0))
            rest = rest - part
        laid = jnp.concatenate(laid, axis=0).astype(BF16)
        lows = jnp.where(low_row == (place & 127), 1.0, 0.0).astype(BF16)
        laid = dot_t(laid, lows)
        laid = laid[0:16] + laid[16:32] + laid[32:48]
        lefts, rights = [], []
        for t in range(SPAN):
            w = laid[t : t + 1]
            tile = base + t
            high, low = halves(perts[tile] * w)
            d_high, d_low = halves(depart[pl.ds(tile, 1), :] * w)
            ends = jnp.concatenate(
                [d_high.astype(F32), d_low.astype(F32), jnp.zeros((14, 128), F32)], axis=0
            )
            lefts.append(jnp.concatenate([high, low, ends.astype(BF16)], axis=0))
            rights.append(parts[tile])
        product = dot_t(jnp.concatenate(lefts, axis=1), jnp.concatenate(rights, axis=1))
        return product

    def fold_first(a, b):
        return a + pltpu.roll(a, MEMBERS, 1) + b

    def fold_second(a, b):
        return a + pltpu.roll(a, MEMBERS, 1) + pltpu.roll(b, MEMBERS, 1)

    def one_pair(k, carry):
        one, two = one_patch(2 * k), one_patch(2 * k + 1)
        both = jnp.where(
            first_half,
            fold_first(one[0:64], one[64:128]),
            fold_second(two[0:64], two[64:128]),
        )
        gram[k] = both + (MEMBERS - 1.0) * unit
        row_one, row_two = one[128:136], two[128:136]
        swapped_one, swapped_two = pltpu.roll(row_one, MEMBERS, 1), pltpu.roll(row_two, MEMBERS, 1)
        end_one = row_one[0:1] + swapped_one[0:1] + row_one[1:2]
        end_two = row_two[0:1] + swapped_two[0:1] + swapped_two[1:2]
        proj[pl.ds(k, 1), :] = jnp.where(first_lane, end_one, end_two)
        return carry

    lax.fori_loop(0, PAIRS, one_pair, 0)

    row128 = lax.broadcasted_iota(jnp.int32, (128, 128), 0)
    lane128 = lax.broadcasted_iota(jnp.int32, (128, 128), 1)
    block_mask = jnp.where((row128 < MEMBERS) == (lane128 < MEMBERS), 1.0, 0.0).astype(BF16)

    def half_sums(value):
        one = jnp.sum(jnp.where(lane64[: value.shape[0]] < MEMBERS, value, 0.0), axis=1, keepdims=True)
        two = jnp.sum(jnp.where(lane64[: value.shape[0]] < MEMBERS, 0.0, value), axis=1, keepdims=True)
        return jnp.where(lane64[: value.shape[0]] < MEMBERS, one, two)

    def batch_of_pairs(batch, carry):
        pairs = [batch * BATCH + i for i in range(BATCH)]
        grams = [gram[k] for k in pairs]
        traces = []
        for g in grams:
            diag = jnp.sum(jnp.where(diagonal, g, 0.0), axis=0, keepdims=True)
            one = jnp.sum(jnp.where(first_lane, diag, 0.0), axis=1, keepdims=True)
            two = jnp.sum(jnp.where(first_lane, 0.0, diag), axis=1, keepdims=True)
            traces.append(jnp.where(first_lane, one, two))
        roots = [g / t for g, t in zip(grams, traces)]
        mids = [1.5 * unit - 0.5 * r for r in roots]
        roots = [folded(dot(left(r), right(m, block_mask))) for r, m in zip(roots, mids)]
        invs = mids

        def sweep(_, state):
            roots, invs = state
            mids = [
                1.5 * unit - 0.5 * folded(dot(left(v), right(r, block_mask)))
                for r, v in zip(roots, invs)
            ]
            new_roots, new_invs = [], []
            for r, v, m in zip(roots, invs, mids):
                both = dot(jnp.concatenate([left(r), left(v)], axis=0), right(m, block_mask))
                new_roots.append(folded(both[0:128]))
                new_invs.append(folded(both[128:256]))
            return new_roots, new_invs

        roots, invs = lax.fori_loop(0, NS_STEPS - 2, sweep, (roots, invs))
        mids = [
            1.5 * unit - 0.5 * folded(dot(left(v), right(r, block_mask)))
            for r, v in zip(roots, invs)
        ]
        invs = [folded(dot(left(v), right(m, block_mask))) for v, m in zip(invs, mids)]

        for k, v, t in zip(pairs, invs, traces):
            factor = right(v, block_mask)
            row = proj[pl.ds(k, 1), :]
            for _ in range(2):
                wide_row = jnp.concatenate([row, jnp.zeros((7, 128), F32)], axis=0)
                row = folded(dot(left(wide_row), factor))[0:1]
            full = v * (math.sqrt(MEMBERS - 1.0) * lax.rsqrt(t)) + row / t
            full = full + (1.0 - half_sums(full)) * (1.0 / MEMBERS)
            weights[k] = full.astype(BF16)
        return carry

    lax.fori_loop(0, PAIRS // BATCH, batch_of_pairs, 0)

    lane_patch = lax.broadcasted_iota(jnp.int32, (16, 128), 1) // 16
    masks = [jnp.where(lane_patch == p, 1.0, 0.0).astype(BF16) for p in range(8)]
    masks = [jnp.concatenate([m] * 4, axis=0) for m in masks]

    for group in range(NG):
        for copy in ins[group]:
            copy.wait()

        def widen(j, carry):
            for v in range(0, NV, 16):
                count = min(16, NV - v)
                wide[pl.ds(j * NVP + v, count), :] = got[group, j, v : v + count].astype(F32)
            return carry

        lax.fori_loop(0, MEMBERS, widen, 0)
        factor = jnp.concatenate([weights[group * 4 + i] for i in range(4)], axis=1)

        def some(first, count):
            fields = []
            for i in range(count):
                field = wide[pl.ds(first + i, MEMBERS, stride=NVP), :].astype(BF16)
                fields.append(jnp.concatenate([field * m for m in masks], axis=0))
            made_here = dot(factor, jnp.concatenate(fields, axis=1))
            for i in range(count):
                wide_out[pl.ds(first + i, MEMBERS, stride=NVP), :] = made_here[:, i * 128 : i * 128 + 128]

        def variables(step, carry):
            some(step * 4, 4)
            return carry

        lax.fori_loop(0, NV // 4, variables, 0)
        some(NV // 4 * 4, NV % 4)

        def narrow(k, carry):
            for v in range(0, NV, 16):
                count = min(16, NV - v)
                made[group, k, v : v + count] = wide_out[pl.ds(k * NVP + v, count), :].astype(BF16)
            return carry

        lax.fori_loop(0, MEMBERS, narrow, 0)
        for copy in outs[group]:
            copy.start()
    for group in range(NG):
        for copy in outs[group]:
            copy.wait()


def on_device(prior, values, quantity, vertical, lists, alive, taper):
    row = ((quantity >> 3) * (BAND // 128) + (vertical >> 7)) * 8 + (quantity & 7)
    spots, columns = row * MINE, vertical & 127
    tiles = jnp.minimum(jnp.min(lists, axis=1) >> 7, NWT - SPAN)
    vmem = pl.BlockSpec(memory_space=pltpu.VMEM)
    smem = pl.BlockSpec(memory_space=pltpu.SMEM)
    dma = pltpu.SemaphoreType.DMA
    peers = len(ORDER)
    return pl.pallas_call(
        kernel,
        out_shape=jax.ShapeDtypeStruct(prior.shape, prior.dtype),
        in_specs=[pl.BlockSpec(memory_space=pl.ANY), smem, smem, smem, smem, vmem, vmem, vmem],
        out_specs=pl.BlockSpec(memory_space=pl.ANY),
        scratch_shapes=[
            pltpu.VMEM((MINE, NV, BAND), BF16),
            pltpu.VMEM((ROWS * MINE, 128), F32),
            pltpu.VMEM((128 * MINE, 128), F32),
            pltpu.VMEM((NG, MEMBERS, NV, 128), BF16),
            pltpu.VMEM((NG, MEMBERS, NV, 128), BF16),
            pltpu.VMEM((NOT * MINE, 128), F32),
            pltpu.VMEM((4, 8 * MINE, 128), BF16),
            pltpu.VMEM((6, MEMBERS // MINE, 8 * MINE, 128), BF16),
            pltpu.VMEM((NWT * MEMBERS, 128), F32),
            pltpu.VMEM((NWT, MEMBERS, 128), F32),
            pltpu.VMEM((6, 8, 128), F32),
            pltpu.VMEM((NWT, 2 * MEMBERS, 128), BF16),
            pltpu.VMEM((NWT, 128), F32),
            pltpu.VMEM((PAIRS, MEMBERS, 128), F32),
            pltpu.VMEM((PAIRS, 128), F32),
            pltpu.VMEM((PAIRS, MEMBERS, 128), BF16),
            pltpu.VMEM((MEMBERS * NVP, 128), F32),
            pltpu.VMEM((MEMBERS * NVP, 128), F32),
            dma((MINE,)),
            dma((NG, peers)), dma((NG, peers)), dma((NG,)),
            dma((peers,)), dma((peers,)), dma,
            dma((2,)), dma((2,)),
            dma((2,)), dma((2,)), dma,
            dma((NG, peers)), dma((NG, peers)), dma((NG,)),
        ],
        compiler_params=pltpu.CompilerParams(
            collective_id=0, has_side_effects=True, vmem_limit_bytes=58 * 2**20
        ),
    )(
        prior,
        spots,
        columns,
        tiles,
        alive[:, 0],
        values.astype(F32).reshape(4, 8, 128),
        lists,
        taper,
    )


def solution(mesh):
    placed = (
        P("mem", None, "lat"),
        P("lat"),
        P("lat"),
        P("lat"),
        P("mem", "lat"),
        P("mem", "lat"),
        P("mem", "lat"),
    )
    return jax.shard_map(
        on_device, mesh=mesh, in_specs=placed, out_specs=P("mem", None, "lat"), check_vma=False
    )
```

time: 418 us -> 183 us (0.44); the launches traced: 410 us -> 183 us
  local copies, waits for them, and re-layouts: 198 us -> 17.3 us
  Pallas kernels: 0 us -> 161 us
  blocking collectives: 101 us -> 0 us
  matrix products: 91.4 us -> 0 us
  starting transfers between devices: 10.7 us -> 0 us
    pallas_call x0 -> x1, Pallas kernels: none -> 161 us  [on_device(): pl.pallas_call(kernel, out_shape=jax.ShapeDtypeStruct(prior.shape, prior....]
    gather x193 -> x0, local copies, waits for them, and re-layouts: 142 us -> none
    dot_general x36 -> x0, matrix products: 91.4 us -> none  [the longest x4 21.6 us: one_patch(): jnp.dot(mean_part[None, :], selector.astype(jnp.float32), precision=lax.P...]
    all_to_all x1 -> x0, blocking collectives: 76.9 us -> none  [on_device(): lax.all_to_all(result, 'mem', split_axis=0, concat_axis=2, tiled=True)]
    reshape x3 -> x0, local copies, waits for them, and re-layouts: 31.7 us -> none  [the longest x1 12.7 us: on_device(): result.astype(jnp.bfloat16)]
    all_gather x1 -> x0, blocking collectives: 24.3 us -> none  [on_device(): every_own = lax.all_gather(equiv, 'mem', axis=0, tiled=True)]
    all_to_all x2 -> x0, local copies, waits for them, and re-layouts: 22.9 us -> none  [the longest x1 17.4 us: on_device(): lax.all_to_all(tile_pieces, 'mem', split_axis=2, concat_axis=0, tiled=True)]
    pallas_call x0 -> x1, local copies, waits for them, and re-layouts: none -> 9.29 us  [on_device(): pl.pallas_call(kernel, out_shape=jax.ShapeDtypeStruct(prior.shape, prior....]
  transfers between devices with their start and end apart: 3 -> 0, of which waited for: 0 -> 0; matrix products, arithmetic and copies ran while one was open for 46% -> 0% of each run, Pallas kernels for 0% -> 0%
where the time goes in v1:
time: 183 us
  Pallas kernels  161 us (88%)
  local copies, waits for them, and re-layouts  17.3 us (9%)
  other arithmetic  4.14 us (2%)
    pallas_call x1, Pallas kernels, on_device(): pl.pallas_call(kernel, out_shape=jax.ShapeDtypeStruct(prior.shape, prior....  161 us
    pallas_call x1, local copies, waits for them, and re-layouts, on_device(): pl.pallas_call(kernel, out_shape=jax.ShapeDtypeStruct(prior.shape, prior....  9.29 us
    unnamed x1, local copies, waits for them, and re-layouts  8.02 us

profile of v1, /device:TPU:96, one launch (start us, length us, event | category | flops | bytes accessed | tf_op | source)
XLA Modules:
  0.0 182.6 jit_solution(8266721213872747604)
XLA Ops:
  0.0 1.0 reduce_min.9
  1.0 0.5 shift-right-arithmetic_minimum_fusion.tiles
  1.5 1.3 bitcast_convert_fusion.values
  2.8 1.3 broadcast_and_fusion
  4.1 8.0 %copy.8.prior = bf16[4,83,8192]{2,1,0:T(8,128)(2,1)} copy(bf16[4,83,8192]{2,0,1:T(4,128)(2,1)} %param.7) | data formatting | bytes 10878976 | tf_op args[0]
  12.2 161.2 %shard_map.73 = bf16[4,83,8192]{2,1,0:T(8,128)(2,1)} custom-call(bf16[4,83,8192]{2,1,0:T(8,128)(2,1)} %copy.8.prior, s32[4096]{0:T(1024)} %get-tuple-element.6.spots, s32[4096]{0:T(1024)} %get-tuple-element.5.columns, s32[32]{0:T(128)} %shift-right-arithmetic_minimum_fusion.tiles, s32[32]{0:T(128)} %bitcast.4, f32[4,8,128]{2,1,0:T(8,128)} %bitcast_convert_fusion.values, ...), custom_call_target="tpu_custom_call" | custom-call | tf_op jit(solution)/shard_map/pallas_call | solution.py:427
  173.4 9.3 %copy.9 = bf16[4,83,8192]{2,0,1:T(4,128)(2,1)} copy(bf16[4,83,8192]{2,1,0:T(8,128)(2,1)} %shard_map.73) | data formatting | bytes 10878976 | tf_op jit(solution)/shard_map/pallas_call | solution.py:427

commit v2 on v1

--- a/solution.py
+++ b/solution.py
@@ -14,10 +14,9 @@
 MEMBERS = 64
 MINE = 4
 NV = 83
-NVP = 88
-BAND = 8192
-OWN = 512
+NCT = 64
 NG = 4
+CHUNKS = ((0, 22), (22, 44), (44, 64), (64, NV))
 PATCHES = 32
 SLOTS = 512
 SPAN = 9
@@ -26,7 +25,8 @@
 NS_STEPS = 8
 PAIRS = PATCHES // 2
 BATCH = 8
-ROWS = (NVP // 8) * (BAND // 128) * 8
+
+EARLY = 1
 
 ORDER = (
     (1, 0), (0, 2), (3, 0), (2, 1), (0, 1), (2, 3), (0, 3), (1, 2),
@@ -69,9 +69,9 @@
 
 
 def kernel(
-    prior, spots, columns, tiles, alive, values, lists, taper,
+    prior, quantity, vertical, alive, values, lists, taper,
     out,
-    mine, table, alone, got, made, equiv32, equiv, every, window, perts, value_win, parts, depart,
+    mine, tiles, values32, alone, got, made, equiv32, equiv, every, window, perts, value_win, parts, depart,
     gram, proj, weights, wide, wide_out,
     own_sem, in_send, in_recv, in_own, gather_send, gather_recv, gather_own,
     halo_send, halo_recv, value_send, value_recv, value_own, out_send, out_recv, out_own,
@@ -82,11 +82,8 @@
     partners = [((my_y + dy) % 4) * 4 + (my_x + dx) % 4 for dx, dy in ORDER]
     north, south = (lat + 1) % bands, (lat + bands - 1) % bands
 
-    load = [
-        pltpu.make_async_copy(prior.at[j], mine.at[j], own_sem.at[j]) for j in range(MINE)
-    ]
-    for copy in load:
-        copy.start()
+    load = pltpu.make_async_copy(prior, mine, own_sem)
+    load.start()
 
     barrier = pltpu.get_barrier_semaphore()
     for partner in partners:
@@ -95,53 +92,55 @@
         pl.semaphore_signal(barrier, inc=1, device_id=(me, band), device_id_type=MESH)
     pl.semaphore_wait(barrier, len(ORDER) + 2)
 
-    def piece(owner, group):
-        return pl.ds(pl.multiple_of(owner * OWN + group * 128, 128), 128)
-
-    my_rows = pl.ds(me * MINE, MINE)
-
-    def copies_in(group):
+    def piece(owner, chunk):
+        return pl.ds(CHUNKS[chunk][0], CHUNKS[chunk][1] - CHUNKS[chunk][0]), pl.ds(owner * NG, NG)
+
+    def block(owner, chunk):
+        return pl.ds(CHUNKS[chunk][0], CHUNKS[chunk][1] - CHUNKS[chunk][0]), owner
+
+    def copies_in(chunk):
         sends = [
             pltpu.make_async_remote_copy(
-                src_ref=prior.at[:, :, piece(partner, group)],
-                dst_ref=got.at[group, my_rows],
-                send_sem=in_send.at[group, s],
-                recv_sem=in_recv.at[group, s],
+                src_ref=prior.at[piece(partner, chunk)],
+                dst_ref=got.at[block(me, chunk)],
+                send_sem=in_send.at[chunk, s],
+                recv_sem=in_recv.at[chunk, s],
                 device_id=(partner, lat),
                 device_id_type=MESH,
             )
             for s, partner in enumerate(partners)
         ]
         own = pltpu.make_async_copy(
-            prior.at[:, :, piece(me, group)], got.at[group, my_rows], in_own.at[group]
+            prior.at[piece(me, chunk)], got.at[block(me, chunk)], in_own.at[chunk]
         )
         return sends + [own]
 
-    def copies_out(group):
+    def copies_out(chunk):
         sends = [
             pltpu.make_async_remote_copy(
-                src_ref=made.at[group, pl.ds(partner * MINE, MINE)],
-                dst_ref=out.at[:, :, piece(me, group)],
-                send_sem=out_send.at[group, s],
-                recv_sem=out_recv.at[group, s],
+                src_ref=made.at[block(partner, chunk)],
+                dst_ref=out.at[piece(me, chunk)],
+                send_sem=out_send.at[chunk, s],
+                recv_sem=out_recv.at[chunk, s],
                 device_id=(partner, lat),
                 device_id_type=MESH,
             )
             for s, partner in enumerate(partners)
         ]
         own = pltpu.make_async_copy(
-            made.at[group, my_rows], out.at[:, :, piece(me, group)], out_own.at[group]
+            made.at[block(me, chunk)], out.at[piece(me, chunk)], out_own.at[chunk]
         )
         return sends + [own]
 
-    ins = [copies_in(group) for group in range(NG)]
-    outs = [copies_out(group) for group in range(NG)]
+    ins = [copies_in(chunk) for chunk in range(len(CHUNKS))]
+    outs = [copies_out(chunk) for chunk in range(len(CHUNKS))]
     for copy in ins[0]:
         copy.start()
 
+    values32[...] = values[...].astype(F32)
     value_copies = [
         pltpu.make_async_remote_copy(
-            src_ref=values.at[source],
+            src_ref=values32.at[source],
             dst_ref=value_win.at[target],
             send_sem=value_send.at[k],
             recv_sem=value_recv.at[k],
@@ -150,36 +149,26 @@
         )
         for k, (source, target, band) in enumerate(((3, 0, north), (0, 5, south)))
     ]
-    value_copies.append(pltpu.make_async_copy(values, value_win.at[pl.ds(1, 4)], value_own))
+    value_copies.append(pltpu.make_async_copy(values32, value_win.at[pl.ds(1, 4)], value_own))
     for copy in value_copies:
         copy.start()
 
-    for copy in load:
-        copy.wait()
-
-    def spread_rows(ct, carry):
-        lanes = pl.ds(pl.multiple_of(ct * 128, 128), 128)
-        for j in range(MINE):
-            for v in range(0, NV, 16):
-                count = min(16, NV - v)
-                block = mine[j, v : v + count, lanes].astype(F32)
-                for t in range(0, count, 8):
-                    n = min(8, count - t)
-                    start = (((v + t) // 8) * (BAND // 128) + ct) * 8 * MINE + j
-                    table[pl.ds(start, n, stride=MINE), :] = block[t : t + n]
+    def first_tile(p, carry):
+        tiles[p] = jnp.minimum(lax.shift_right_logical(jnp.min(lists[pl.ds(p, 1), :]), 7), NWT - SPAN)
         return carry
 
-    lax.fori_loop(0, BAND // 128, spread_rows, 0)
+    lax.fori_loop(0, PATCHES, first_tile, 0)
 
     lane4 = lax.broadcasted_iota(jnp.int32, (MINE, 128), 1)
     ones = jnp.ones((8, 128), BF16)
 
+    load.wait()
+
     def pick(ot, carry):
         for i in range(128):
-            found = table[pl.ds(spots[ot * 128 + i], MINE), :]
-            alone[pl.ds(i, MINE, stride=128), :] = jnp.where(
-                lane4 == columns[ot * 128 + i], found, 0.0
-            )
+            column = vertical[ot * 128 + i]
+            found = mine[quantity[ot * 128 + i], lax.shift_right_logical(column, 7)].astype(F32)
+            alone[pl.ds(i, MINE, stride=128), :] = jnp.where(lane4 == (column & 127), found, 0.0)
         row = dot_t(ones, alone[...].astype(BF16))
         start = (ot // 8) * 8 * MINE + ot % 8
         for j in range(MINE):
@@ -190,22 +179,48 @@
     for quarter in range(4):
         equiv[quarter] = equiv32[quarter * 32 : quarter * 32 + 32].astype(BF16)
 
-    gathers = [
-        pltpu.make_async_remote_copy(
-            src_ref=equiv,
-            dst_ref=every.at[pl.ds(1, 4), me],
-            send_sem=gather_send.at[s],
-            recv_sem=gather_recv.at[s],
+    side_x = [my_y * 4 + (my_x + d) % 4 for d in (1, 3, 2)]
+    side_y = [((my_y + d) % 4) * 4 + my_x for d in (1, 3, 2)]
+    first, second = pl.ds(1, 2), pl.ds(3, 2)
+
+    def gather(source, target, k, partner):
+        return pltpu.make_async_remote_copy(
+            src_ref=source,
+            dst_ref=target,
+            send_sem=gather_send.at[k],
+            recv_sem=gather_recv.at[k],
             device_id=(partner, lat),
             device_id_type=MESH,
         )
-        for s, partner in enumerate(partners)
-    ]
-    gathers.append(pltpu.make_async_copy(equiv, every.at[pl.ds(1, 4), me], gather_own))
+
+    gathers = [
+        gather(equiv.at[pl.ds(0, 2)], every.at[first, my_y, my_x], k, partner)
+        for k, partner in enumerate(side_x)
+    ]
+    gathers += [
+        gather(equiv.at[pl.ds(2, 2)], every.at[second, my_y, my_x], 3 + k, partner)
+        for k, partner in enumerate(side_y)
+    ]
+    gathers.append(pltpu.make_async_copy(equiv, every.at[pl.ds(1, 4), my_y, my_x], gather_own))
     for copy in gathers:
         copy.start()
-    for group in range(1, NG):
-        for copy in ins[group]:
+    for chunk in range(1, EARLY):
+        for copy in ins[chunk]:
+            copy.start()
+    for copy in gathers:
+        copy.wait()
+    gathers = [
+        gather(every.at[first, my_y], every.at[first, my_y], 6 + k, partner)
+        for k, partner in enumerate(side_y)
+    ]
+    gathers += [
+        gather(every.at[second, :, my_x], every.at[second, :, my_x], 9 + k, partner)
+        for k, partner in enumerate(side_x)
+    ]
+    for copy in gathers:
+        copy.start()
+    for chunk in range(EARLY, len(CHUNKS)):
+        for copy in ins[chunk]:
             copy.start()
     for copy in gathers:
         copy.wait()
@@ -225,7 +240,7 @@
 
     def spread_members(q, carry):
         for m in range(MEMBERS // MINE):
-            block = every[q, m].astype(F32)
+            block = every[q, m // 4, m % 4].astype(F32)
             for j in range(MINE):
                 start = q * 8 * MEMBERS + m * MINE + j
                 window[pl.ds(start, 8, stride=MEMBERS), :] = block[j * 8 : j * 8 + 8]
@@ -369,75 +384,91 @@
 
     lax.fori_loop(0, PAIRS // BATCH, batch_of_pairs, 0)
 
-    lane_patch = lax.broadcasted_iota(jnp.int32, (16, 128), 1) // 16
+    lane_patch = lax.broadcasted_iota(jnp.int32, (MEMBERS, 128), 1) // 16
     masks = [jnp.where(lane_patch == p, 1.0, 0.0).astype(BF16) for p in range(8)]
-    masks = [jnp.concatenate([m] * 4, axis=0) for m in masks]
-
-    for group in range(NG):
-        for copy in ins[group]:
-            copy.wait()
-
-        def widen(j, carry):
-            for v in range(0, NV, 16):
-                count = min(16, NV - v)
-                wide[pl.ds(j * NVP + v, count), :] = got[group, j, v : v + count].astype(F32)
-            return carry
-
-        lax.fori_loop(0, MEMBERS, widen, 0)
-        factor = jnp.concatenate([weights[group * 4 + i] for i in range(4)], axis=1)
-
-        def some(first, count):
+    factors = [
+        jnp.concatenate([weights[group * 4 + i] for i in range(4)], axis=1) for group in range(NG)
+    ]
+
+    def some(first, count):
+        for group in range(NG):
+            for i in range(count):
+                for m in range(MEMBERS // MINE):
+                    wide[group, i, m * MINE : m * MINE + MINE] = got[first + i, m, group].astype(F32)
+        for group in range(NG):
             fields = []
             for i in range(count):
-                field = wide[pl.ds(first + i, MEMBERS, stride=NVP), :].astype(BF16)
+                field = wide[group, i].astype(BF16)
                 fields.append(jnp.concatenate([field * m for m in masks], axis=0))
-            made_here = dot(factor, jnp.concatenate(fields, axis=1))
+            result = dot(factors[group], jnp.concatenate(fields, axis=1))
             for i in range(count):
-                wide_out[pl.ds(first + i, MEMBERS, stride=NVP), :] = made_here[:, i * 128 : i * 128 + 128]
-
-        def variables(step, carry):
-            some(step * 4, 4)
+                wide_out[group, i] = result[:, i * 128 : i * 128 + 128]
+        for group in range(NG):
+            for i in range(count):
+                for m in range(MEMBERS // MINE):
+                    made[first + i, m, group] = wide_out[
+                        group, i, m * MINE : m * MINE + MINE
+                    ].astype(BF16)
+
+    for chunk, (start, stop) in enumerate(CHUNKS):
+        for copy in ins[chunk]:
+            copy.wait()
+
+        def variables(step, carry, start=start):
+            some(start + step * 2, 2)
             return carry
 
-        lax.fori_loop(0, NV // 4, variables, 0)
-        some(NV // 4 * 4, NV % 4)
-
-        def narrow(k, carry):
-            for v in range(0, NV, 16):
-                count = min(16, NV - v)
-                made[group, k, v : v + count] = wide_out[pl.ds(k * NVP + v, count), :].astype(BF16)
-            return carry
-
-        lax.fori_loop(0, MEMBERS, narrow, 0)
-        for copy in outs[group]:
+        lax.fori_loop(0, (stop - start) // 2, variables, 0)
+        if (stop - start) % 2:
+            some(stop - 1, 1)
+        for copy in outs[chunk]:
             copy.start()
-    for group in range(NG):
-        for copy in outs[group]:
+    for chunk in range(len(CHUNKS)):
+        for copy in outs[chunk]:
             copy.wait()
 
 
+def keeper(made, out, held, reads, writes):
+    parts = [pl.ds(start, stop - start) for start, stop in CHUNKS]
+    copies_in = [
+        pltpu.make_async_copy(made.at[part], held.at[part], reads.at[k])
+        for k, part in enumerate(parts)
+    ]
+    copies_out = [
+        pltpu.make_async_copy(held.at[part], out.at[part], writes.at[k])
+        for k, part in enumerate(parts)
+    ]
+    for copy in copies_in:
+        copy.start()
+    for read, write in zip(copies_in, copies_out):
+        read.wait()
+        write.start()
+    for copy in copies_out:
+        copy.wait()
+
+
 def on_device(prior, values, quantity, vertical, lists, alive, taper):
-    row = ((quantity >> 3) * (BAND // 128) + (vertical >> 7)) * 8 + (quantity & 7)
-    spots, columns = row * MINE, vertical & 127
-    tiles = jnp.minimum(jnp.min(lists, axis=1) >> 7, NWT - SPAN)
     vmem = pl.BlockSpec(memory_space=pltpu.VMEM)
     smem = pl.BlockSpec(memory_space=pltpu.SMEM)
     dma = pltpu.SemaphoreType.DMA
-    peers = len(ORDER)
-    return pl.pallas_call(
+    peers, chunks = len(ORDER), len(CHUNKS)
+    shape = (NV, NCT, MINE, 128)
+    prior = prior.reshape(MINE, NV, NCT, 128).transpose(1, 2, 0, 3)
+    result = pl.pallas_call(
         kernel,
-        out_shape=jax.ShapeDtypeStruct(prior.shape, prior.dtype),
-        in_specs=[pl.BlockSpec(memory_space=pl.ANY), smem, smem, smem, smem, vmem, vmem, vmem],
+        out_shape=jax.ShapeDtypeStruct(shape, prior.dtype),
+        in_specs=[pl.BlockSpec(memory_space=pl.ANY), smem, smem, smem, vmem, vmem, vmem],
         out_specs=pl.BlockSpec(memory_space=pl.ANY),
         scratch_shapes=[
-            pltpu.VMEM((MINE, NV, BAND), BF16),
-            pltpu.VMEM((ROWS * MINE, 128), F32),
+            pltpu.VMEM((NV, NCT, MINE, 128), BF16),
+            pltpu.SMEM((PATCHES,), jnp.int32),
+            pltpu.VMEM((4, 8, 128), F32),
             pltpu.VMEM((128 * MINE, 128), F32),
-            pltpu.VMEM((NG, MEMBERS, NV, 128), BF16),
-            pltpu.VMEM((NG, MEMBERS, NV, 128), BF16),
+            pltpu.VMEM((NV, MEMBERS // MINE, NG, MINE, 128), BF16),
+            pltpu.VMEM((NV, MEMBERS // MINE, NG, MINE, 128), BF16),
             pltpu.VMEM((NOT * MINE, 128), F32),
             pltpu.VMEM((4, 8 * MINE, 128), BF16),
-            pltpu.VMEM((6, MEMBERS // MINE, 8 * MINE, 128), BF16),
+            pltpu.VMEM((6, 4, 4, 8 * MINE, 128), BF16),
             pltpu.VMEM((NWT * MEMBERS, 128), F32),
             pltpu.VMEM((NWT, MEMBERS, 128), F32),
             pltpu.VMEM((6, 8, 128), F32),
@@ -446,28 +477,36 @@
             pltpu.VMEM((PAIRS, MEMBERS, 128), F32),
             pltpu.VMEM((PAIRS, 128), F32),
             pltpu.VMEM((PAIRS, MEMBERS, 128), BF16),
-            pltpu.VMEM((MEMBERS * NVP, 128), F32),
-            pltpu.VMEM((MEMBERS * NVP, 128), F32),
-            dma((MINE,)),
-            dma((NG, peers)), dma((NG, peers)), dma((NG,)),
-            dma((peers,)), dma((peers,)), dma,
+            pltpu.VMEM((NG, 2, MEMBERS, 128), F32),
+            pltpu.VMEM((NG, 2, MEMBERS, 128), F32),
+            dma,
+            dma((chunks, peers)), dma((chunks, peers)), dma((chunks,)),
+            dma((12,)), dma((12,)), dma,
             dma((2,)), dma((2,)),
             dma((2,)), dma((2,)), dma,
-            dma((NG, peers)), dma((NG, peers)), dma((NG,)),
+            dma((chunks, peers)), dma((chunks, peers)), dma((chunks,)),
         ],
         compiler_params=pltpu.CompilerParams(
             collective_id=0, has_side_effects=True, vmem_limit_bytes=58 * 2**20
         ),
     )(
         prior,
-        spots,
-        columns,
-        tiles,
+        quantity,
+        vertical,
         alive[:, 0],
-        values.astype(F32).reshape(4, 8, 128),
+        values.reshape(4, 8, 128),
         lists,
         taper,
     )
+    result = pl.pallas_call(
+        keeper,
+        out_shape=jax.ShapeDtypeStruct(shape, prior.dtype),
+        in_specs=[pl.BlockSpec(memory_space=pl.ANY)],
+        out_specs=pl.BlockSpec(memory_space=pl.ANY),
+        scratch_shapes=[pltpu.VMEM(shape, BF16), dma((chunks,)), dma((chunks,))],
+        compiler_params=pltpu.CompilerParams(vmem_limit_bytes=58 * 2**20),
+    )(result)
+    return result.transpose(2, 0, 1, 3).reshape(MINE, NV, NCT * 128)
 
 
 def solution(mesh):

time: 183 us -> 150 us (0.82)
  local copies, waits for them, and re-layouts: 17.3 us -> 0 us
  Pallas kernels: 161 us -> 150 us
  other arithmetic: 4.14 us -> 0 us
    pallas_call x1 -> x2, Pallas kernels: 161 us -> 150 us  [the longest x1 146 us: on_device(): pl.pallas_call(kernel, out_shape=jax.ShapeDtypeStruct(shape, prior.dtype)...]
    pallas_call x1 -> x0, local copies, waits for them, and re-layouts: 9.29 us -> none  [on_device(): pl.pallas_call(kernel, out_shape=jax.ShapeDtypeStruct(prior.shape, prior....]
    unnamed x1 -> x0, local copies, waits for them, and re-layouts: 8.02 us -> none
where the time goes in v2:
time: 150 us
  Pallas kernels  150 us (100%)
    pallas_call x1, Pallas kernels, on_device(): pl.pallas_call(kernel, out_shape=jax.ShapeDtypeStruct(shape, prior.dtype)...  146 us
    pallas_call x1, Pallas kernels, on_device(): pl.pallas_call(keeper, out_shape=jax.ShapeDtypeStruct(shape, prior.dtype)...  4.27 us

profile of v2, /device:TPU:96, one launch (start us, length us, event | category | flops | bytes accessed | tf_op | source)
XLA Modules:
  0.0 150.2 jit_solution(12049105982095326030)
XLA Ops:
  0.0 145.9 %shard_map.73.made = bf16[83,64,4,128]{3,2,1,0:T(4,128)(2,1)} custom-call(bf16[83,64,4,128]{3,2,1,0:T(4,128)(2,1)} %bitcast.8, s32[4096]{0:T(1024)} %quantity.1, s32[4096]{0:T(1024)} %vertical.1, s32[32]{0:T(128)} %bitcast.10, bf16[4,8,128]{2,1,0:T(8,128)(2,1)} %bitcast.9, s32[32,512]{1,0:T(8,128)} %lists.1, f32[32,512]{1,0:T(8,128)} %taper.1), custom_call_target="tpu_custom_call" | custom-call | tf_op jit(solution)/shard_map/pallas_call | solution.py:457
  145.9 4.3 %shard_map.74 = bf16[83,64,4,128]{3,2,1,0:T(4,128)(2,1)} custom-call(bf16[83,64,4,128]{3,2,1,0:T(4,128)(2,1)} %shard_map.73.made), custom_call_target="tpu_custom_call" | custom-call | tf_op jit(solution)/shard_map/pallas_call | solution.py:501

commit v3 on v2

--- a/solution.py
+++ b/solution.py
@@ -15,8 +15,9 @@
 MINE = 4
 NV = 83
 NCT = 64
+BAND = NCT * 128
 NG = 4
-CHUNKS = ((0, 22), (22, 44), (44, 64), (64, NV))
+CHUNKS = tuple((NV * i // 8, NV * (i + 1) // 8) for i in range(8))
 PATCHES = 32
 SLOTS = 512
 SPAN = 9
@@ -24,13 +25,15 @@
 NOT = 32
 NS_STEPS = 8
 PAIRS = PATCHES // 2
-BATCH = 8
-
-EARLY = 1
+BATCH = 16
+
+KEEP = 4
+FIRST = 2
+EARLY = 3
 
 ORDER = (
-    (1, 0), (0, 2), (3, 0), (2, 1), (0, 1), (2, 3), (0, 3), (1, 2),
-    (2, 0), (3, 2), (1, 1), (3, 3), (2, 2), (1, 3), (3, 1),
+    (2, 2), (2, 3), (3, 2), (1, 2), (2, 1), (3, 3), (1, 3), (0, 2),
+    (3, 1), (1, 1), (2, 0), (0, 3), (0, 1), (3, 0), (1, 0),
 )
 
 
@@ -69,7 +72,7 @@
 
 
 def kernel(
-    prior, quantity, vertical, alive, values, lists, taper,
+    prior, flat, codes, alive, values, lists, taper,
     out,
     mine, tiles, values32, alone, got, made, equiv32, equiv, every, window, perts, value_win, parts, depart,
     gram, proj, weights, wide, wide_out,
@@ -79,10 +82,13 @@
     me, lat = lax.axis_index("mem"), lax.axis_index("lat")
     bands = lax.axis_size("lat")
     my_y, my_x = me // 4, me % 4
-    partners = [((my_y + dy) % 4) * 4 + (my_x + dx) % 4 for dx, dy in ORDER]
+    turn = 1 - 2 * (lat % 2)
+    partners = [
+        ((my_y + turn * dy + 4) % 4) * 4 + (my_x + turn * dx + 4) % 4 for dx, dy in ORDER
+    ]
     north, south = (lat + 1) % bands, (lat + bands - 1) % bands
 
-    load = pltpu.make_async_copy(prior, mine, own_sem)
+    load = pltpu.make_async_copy(flat, mine, own_sem)
     load.start()
 
     barrier = pltpu.get_barrier_semaphore()
@@ -134,8 +140,9 @@
 
     ins = [copies_in(chunk) for chunk in range(len(CHUNKS))]
     outs = [copies_out(chunk) for chunk in range(len(CHUNKS))]
-    for copy in ins[0]:
-        copy.start()
+    for chunk in range(FIRST):
+        for copy in ins[chunk]:
+            copy.start()
 
     values32[...] = values[...].astype(F32)
     value_copies = [
@@ -153,12 +160,6 @@
     for copy in value_copies:
         copy.start()
 
-    def first_tile(p, carry):
-        tiles[p] = jnp.minimum(lax.shift_right_logical(jnp.min(lists[pl.ds(p, 1), :]), 7), NWT - SPAN)
-        return carry
-
-    lax.fori_loop(0, PATCHES, first_tile, 0)
-
     lane4 = lax.broadcasted_iota(jnp.int32, (MINE, 128), 1)
     ones = jnp.ones((8, 128), BF16)
 
@@ -166,10 +167,11 @@
 
     def pick(ot, carry):
         for i in range(128):
-            column = vertical[ot * 128 + i]
-            found = mine[quantity[ot * 128 + i], lax.shift_right_logical(column, 7)].astype(F32)
-            alone[pl.ds(i, MINE, stride=128), :] = jnp.where(lane4 == (column & 127), found, 0.0)
-        row = dot_t(ones, alone[...].astype(BF16))
+            code = codes[ot * 128 + i]
+            found = mine[lax.shift_right_logical(code, 7)].astype(F32)
+            alone[i * MINE : i * MINE + MINE] = jnp.where(lane4 == (code & 127), found, 0.0)
+        sorted_rows = [alone[pl.ds(j, 128, stride=MINE), :].astype(BF16) for j in range(MINE)]
+        row = dot_t(ones, jnp.concatenate(sorted_rows, axis=0))
         start = (ot // 8) * 8 * MINE + ot % 8
         for j in range(MINE):
             equiv32[pl.ds(start + j * 8, 1), :] = row[0:1, j * 128 : j * 128 + 128]
@@ -204,9 +206,15 @@
     gathers.append(pltpu.make_async_copy(equiv, every.at[pl.ds(1, 4), my_y, my_x], gather_own))
     for copy in gathers:
         copy.start()
-    for chunk in range(1, EARLY):
+    for chunk in range(FIRST, EARLY):
         for copy in ins[chunk]:
             copy.start()
+    def first_tile(p, carry):
+        tiles[p] = jnp.minimum(lax.shift_right_logical(jnp.min(lists[pl.ds(p, 1), :]), 7), NWT - SPAN)
+        return carry
+
+    lax.fori_loop(0, PATCHES, first_tile, 0)
+
     for copy in gathers:
         copy.wait()
     gathers = [
@@ -428,22 +436,17 @@
             copy.wait()
 
 
-def keeper(made, out, held, reads, writes):
-    parts = [pl.ds(start, stop - start) for start, stop in CHUNKS]
-    copies_in = [
-        pltpu.make_async_copy(made.at[part], held.at[part], reads.at[k])
-        for k, part in enumerate(parts)
-    ]
-    copies_out = [
-        pltpu.make_async_copy(held.at[part], out.at[part], writes.at[k])
-        for k, part in enumerate(parts)
-    ]
-    for copy in copies_in:
+def keeper(made, out, writes):
+    bounds = [NV * i // KEEP for i in range(KEEP + 1)]
+    copies = [
+        pltpu.make_async_copy(
+            made.at[pl.ds(start, stop - start)], out.at[pl.ds(start, stop - start)], writes.at[k]
+        )
+        for k, (start, stop) in enumerate(zip(bounds, bounds[1:]))
+    ]
+    for copy in copies:
         copy.start()
-    for read, write in zip(copies_in, copies_out):
-        read.wait()
-        write.start()
-    for copy in copies_out:
+    for copy in copies:
         copy.wait()
 
 
@@ -456,11 +459,11 @@
     prior = prior.reshape(MINE, NV, NCT, 128).transpose(1, 2, 0, 3)
     result = pl.pallas_call(
         kernel,
-        out_shape=jax.ShapeDtypeStruct(shape, prior.dtype),
-        in_specs=[pl.BlockSpec(memory_space=pl.ANY), smem, smem, smem, vmem, vmem, vmem],
-        out_specs=pl.BlockSpec(memory_space=pl.ANY),
+        out_shape=pltpu.VMEM(shape, prior.dtype),
+        in_specs=[pl.BlockSpec(memory_space=pl.ANY)] * 2 + [smem, smem, vmem, vmem, vmem],
+        out_specs=pl.BlockSpec(memory_space=pltpu.VMEM),
         scratch_shapes=[
-            pltpu.VMEM((NV, NCT, MINE, 128), BF16),
+            pltpu.VMEM((NV * NCT, MINE, 128), BF16),
             pltpu.SMEM((PATCHES,), jnp.int32),
             pltpu.VMEM((4, 8, 128), F32),
             pltpu.VMEM((128 * MINE, 128), F32),
@@ -487,12 +490,12 @@
             dma((chunks, peers)), dma((chunks, peers)), dma((chunks,)),
         ],
         compiler_params=pltpu.CompilerParams(
-            collective_id=0, has_side_effects=True, vmem_limit_bytes=58 * 2**20
+            collective_id=0, has_side_effects=True, vmem_limit_bytes=54 * 2**20
         ),
     )(
         prior,
-        quantity,
-        vertical,
+        prior.reshape(NV * NCT, MINE, 128),
+        quantity * BAND + vertical,
         alive[:, 0],
         values.reshape(4, 8, 128),
         lists,
@@ -501,10 +504,10 @@
     result = pl.pallas_call(
         keeper,
         out_shape=jax.ShapeDtypeStruct(shape, prior.dtype),
-        in_specs=[pl.BlockSpec(memory_space=pl.ANY)],
+        in_specs=[pl.BlockSpec(memory_space=pltpu.VMEM)],
         out_specs=pl.BlockSpec(memory_space=pl.ANY),
-        scratch_shapes=[pltpu.VMEM(shape, BF16), dma((chunks,)), dma((chunks,))],
-        compiler_params=pltpu.CompilerParams(vmem_limit_bytes=58 * 2**20),
+        scratch_shapes=[dma((KEEP,))],
+        compiler_params=pltpu.CompilerParams(vmem_limit_bytes=16 * 2**20),
     )(result)
     return result.transpose(2, 0, 1, 3).reshape(MINE, NV, NCT * 128)
 

time: 150 us -> 142 us (0.947)
  Pallas kernels: 150 us -> 140 us
    pallas_call x1, Pallas kernels: 146 us -> 138 us  [on_device(): pl.pallas_call(kernel, out_shape=pltpu.VMEM(shape, prior.dtype), in_specs...]
    pallas_call x1, Pallas kernels: 4.27 us -> 2.45 us  [on_device(): pl.pallas_call(keeper, out_shape=jax.ShapeDtypeStruct(shape, prior.dtype)...]
where the time goes in v3:
time: 142 us
  Pallas kernels  140 us (99%)
    pallas_call x1, Pallas kernels, on_device(): pl.pallas_call(kernel, out_shape=pltpu.VMEM(shape, prior.dtype), in_specs...  138 us

profile of v3, /device:TPU:96, one launch (start us, length us, event | category | flops | bytes accessed | tf_op | source)
XLA Modules:
  0.0 141.8 jit_solution(17511047143152605305)
XLA Ops:
  0.0 1.3 multiply_add_fusion.codes
  1.3 138.0 %shard_map.73.made = bf16[83,64,4,128]{3,2,1,0:T(4,128)(2,1)S(1)} custom-call(bf16[83,64,4,128]{3,2,1,0:T(4,128)(2,1)} %bitcast.10, bf16[5312,4,128]{2,1,0:T(4,128)(2,1)} %bitcast.11, s32[4096]{0:T(1024)} %multiply_add_fusion.codes, s32[32]{0:T(128)} %bitcast.13, bf16[4,8,128]{2,1,0:T(8,128)(2,1)} %bitcast.12, s32[32,512]{1,0:T(8,128)} %lists.1, f32[32,512]{1,0:T(8,128)} %taper.1), custom_call_target="tpu_custom_call" | custom-call | tf_op jit(solution)/shard_map/pallas_call | solution.py:460
  139.4 2.5 %shard_map.74 = bf16[83,64,4,128]{3,2,1,0:T(4,128)(2,1)} custom-call(bf16[83,64,4,128]{3,2,1,0:T(4,128)(2,1)S(1)} %shard_map.73.made), custom_call_target="tpu_custom_call" | custom-call | tf_op jit(solution)/shard_map/pallas_call | solution.py:504

commit v4 on v3

--- a/solution.py
+++ b/solution.py
@@ -213,7 +213,7 @@
         tiles[p] = jnp.minimum(lax.shift_right_logical(jnp.min(lists[pl.ds(p, 1), :]), 7), NWT - SPAN)
         return carry
 
-    lax.fori_loop(0, PATCHES, first_tile, 0)
+    lax.fori_loop(0, PATCHES, first_tile, 0, unroll=8)
 
     for copy in gathers:
         copy.wait()

time: 142 us -> 142 us (level)
  no operation moved by 1% of the time
where the time goes in v4:
time: 142 us
  Pallas kernels  140 us (99%)
    pallas_call x1, Pallas kernels, on_device(): pl.pallas_call(kernel, out_shape=pltpu.VMEM(shape, prior.dtype), in_specs...  138 us

profile of v4, /device:TPU:96, one launch (start us, length us, event | category | flops | bytes accessed | tf_op | source)
XLA Modules:
  0.0 141.8 jit_solution(12015899001719859110)
XLA Ops:
  0.0 1.3 multiply_add_fusion.codes
  1.3 138.0 %shard_map.73.made = bf16[83,64,4,128]{3,2,1,0:T(4,128)(2,1)S(1)} custom-call(bf16[83,64,4,128]{3,2,1,0:T(4,128)(2,1)} %bitcast.10, bf16[5312,4,128]{2,1,0:T(4,128)(2,1)} %bitcast.11, s32[4096]{0:T(1024)} %multiply_add_fusion.codes, s32[32]{0:T(128)} %bitcast.13, bf16[4,8,128]{2,1,0:T(8,128)(2,1)} %bitcast.12, s32[32,512]{1,0:T(8,128)} %lists.1, f32[32,512]{1,0:T(8,128)} %taper.1), custom_call_target="tpu_custom_call" | custom-call | tf_op jit(solution)/shard_map/pallas_call | solution.py:460
  139.4 2.5 %shard_map.74 = bf16[83,64,4,128]{3,2,1,0:T(4,128)(2,1)} custom-call(bf16[83,64,4,128]{3,2,1,0:T(4,128)(2,1)S(1)} %shard_map.73.made), custom_call_target="tpu_custom_call" | custom-call | tf_op jit(solution)/shard_map/pallas_call | solution.py:504
